TPU v7x, 32 devices: a whole 2x2x4 slice. The times are simulated.
32 devices in a mesh: grp: 2 (over x), row: 8 (over z, y), col: 2 (over core).
Axes of the slice: x: 2, y: 2, z: 4, core: 2. Of those that a mesh axis runs over, the one named last changes fastest.
Arguments:
- pair_grid: bfloat16 [256, 128, 128], P(('grp', 'row'), 'col'), parts along dimension 0, may hold values from -6 to 6
- token_mask: int32 [256], P('grp'), parts along dimension 0, may hold values 0 or 1
- proj_weight: bfloat16 [128, 512], replicated, may hold values from -0.5 to 0.5
- gate_weight: bfloat16 [128, 128], replicated, may hold values from -0.5 to 0.5
- out_weight: bfloat16 [128, 128], replicated, may hold values from -0.5 to 0.5
- in_gain: float32 [128], replicated, may hold values from 0.5 to 1.5
- out_gain: float32 [128], replicated, may hold values from 0.5 to 1.5
Outputs:
- update: bfloat16 [256, 128, 128], P(('grp', 'row'), 'col'), parts along dimension 0
There are 2 independent parts, one for each index of `grp`. A program takes and returns all parts, laid end to end along the dimension named above; an argument that names none is the same for every part. Nothing has to cross between parts.
All inputs are finite; a program needn't handle non-finite values.
Results may differ from a plain program's by a relative error of at most 0.0079.
Values may be sent and summed in bfloat16 or wider, within the bound.
A program may use at most 128 MiB of HBM per device.

v0:
```python
import jax
import jax.numpy as jnp
from jax import lax
from jax.sharding import PartitionSpec as P


def layer_norm(inputs, scales, along):
    centre = jnp.mean(inputs, axis=along, keepdims=True)
    shifted = inputs - centre
    spread = jnp.mean(shifted * shifted, axis=along, keepdims=True)
    return shifted * lax.rsqrt(spread + 1e-05) * scales


def body(pair_grid, token_mask, proj_weight, gate_weight, out_weight, in_gain, out_gain):
    row_count, col_count, channels = pair_grid.shape
    row_offset = lax.axis_index("row") * row_count
    col_offset = lax.axis_index("col") * col_count
    row_valid = lax.dynamic_slice_in_dim(token_mask, row_offset, row_count).astype(jnp.float32)
    col_valid = lax.dynamic_slice_in_dim(token_mask, col_offset, col_count).astype(jnp.float32)
    normed = layer_norm(pair_grid.astype(jnp.float32), in_gain, -1).astype(jnp.bfloat16)
    flat_cells = normed.reshape(-1, channels)
    projected = jnp.dot(flat_cells, proj_weight, preferred_element_type=jnp.float32).reshape(
        row_count, col_count, 4 * channels
    )
    pair_mask = (row_valid[:, None] * col_valid[None, :])[..., None]
    left_side = (
        pair_mask
        * jax.nn.sigmoid(projected[..., :channels])
        * projected[..., channels : 2 * channels]
    ).astype(jnp.bfloat16)
    right_side = (
        pair_mask
        * jax.nn.sigmoid(projected[..., 2 * channels : 3 * channels])
        * projected[..., 3 * channels :]
    ).astype(jnp.bfloat16)
    out_gate = jax.nn.sigmoid(
        jnp.dot(flat_cells, gate_weight, preferred_element_type=jnp.float32)
    ).reshape(row_count, col_count, channels)
    left_major = jnp.transpose(left_side, (2, 0, 1))
    right_major = jnp.transpose(right_side, (2, 0, 1))
    partial_sum = jnp.einsum(
        "cik,cjk->cij",
        left_major,
        lax.all_gather(right_major, "row", axis=1, tiled=True),
        preferred_element_type=jnp.float32,
    )
    summed = lax.psum_scatter(partial_sum, "col", scatter_dimension=2, tiled=True)
    normed_out = layer_norm(summed, out_gain[:, None, None], 0).astype(jnp.bfloat16)
    normed_cells = jnp.transpose(normed_out, (1, 2, 0))
    projected_out = jnp.dot(
        normed_cells.reshape(-1, channels), out_weight, preferred_element_type=jnp.float32
    ).reshape(row_count, col_count, channels)
    return (out_gate * projected_out).astype(jnp.bfloat16)


def solution(mesh):
    placed = (P(("grp", "row"), "col", None), P("grp"), P(), P(), P(), P(), P())
    return jax.shard_map(
        body, mesh=mesh, in_specs=placed, out_specs=P(("grp", "row"), "col", None), check_vma=False
    )
```

profile of v0, /device:TPU:1, one launch (start us, length us, event | category | flops | bytes accessed | tf_op | source)
XLA Modules:
  0.0 98.1 jit_solution(17692791364899948991)
XLA Ops:
  6.5 0.0 copy-start
  6.5 0.0 all-gather.2.cloned.1.call-start
  6.5 0.8 dynamic-slice_convert_fusion.1
  7.3 0.7 dynamic-slice_convert_fusion
  8.0 1.2 %convert_reduce_fusion = f32[16,64]{1,0:T(8,128)S(1)} fusion(bf16[16,64,128]{2,1,0:T(8,128)(2,1)} %param.7), kind=kLoop, calls=%fused_computation.7 | loop fusion | flops 261120 | bytes 266240 | tf_op jit(solution)/shard_map/reduce_sum | solution.py:8
  9.2 1.3 %fusion.6 = f32[16,64]{1,0:T(8,128)S(1)} fusion(bf16[16,64,128]{2,1,0:T(8,128)(2,1)} %param.7, f32[16,64]{1,0:T(8,128)S(1)} %broadcast_multiply_fusion.2), kind=kLoop, calls=%fused_computation.10 | loop fusion | flops 523264 | bytes 270336 | tf_op jit(solution)/shard_map/reduce_sum | solution.py:10
  10.6 0.1 broadcast_multiply_fusion
  10.6 1.3 %fusion.8 = bf16[16,64,128]{2,1,0:T(8,128)(2,1)S(1)} fusion(bf16[16,64,128]{2,1,0:T(8,128)(2,1)} %param.7, f32[128]{0:T(128)} %param.12, f32[16,64]{1,0:T(8,128)S(1)} %add_rsqrt_fusion.1, f32[16,64]{1,0:T(8,128)S(1)} %broadcast_multiply_fusion.2), kind=kLoop, calls=%fused_computation.12 | loop fusion | flops 655360 | bytes 532992 | tf_op jit(solution)/shard_map/convert_element_type | solution.py:20
  11.9 0.0 copy-done
  11.9 0.4 fusion.23
  12.4 1.0 %fusion.22 = (bf16[128,16,64]{0,2,1:T(8,128)(2,1)}, bf16[128,16,64]{0,2,1:T(8,128)(2,1)S(1)}) fusion(f32[16,64,512]{2,1,0:T(8,128)S(1)} %fusion.23, f32[16,64]{1,0:T(8,128)S(1)} %broadcast_multiply_fusion), kind=kLoop, calls=%fused_computation.32 | loop fusion | flops 1572864 | bytes 2625536 | tf_op jit(solution)/shard_map/transpose | solution.py:40
  13.4 0.0 all-gather.2.cloned.1.call-update
  13.4 0.0 reduce-scatter.2.cloned.1.call-start
  13.5 0.4 copy.23
  13.9 49.9 %all-gather.2.cloned.1.call-done = bf16[128,128,64]{0,2,1:T(8,128)(2,1)} async-done(((bf16[128,16,64]{0,2,1:T(8,128)(2,1)}), bf16[128,128,64]{0,2,1:T(8,128)(2,1)}) %all-gather.2.cloned.1.call-update) | async-done | bytes 2097168 | tf_op jit(solution)/shard_map/all_gather | solution.py:44
  63.8 7.4 %copy.24 = bf16[128,128,64]{2,1,0:T(8,128)(2,1)} copy(bf16[128,128,64]{0,2,1:T(8,128)(2,1)} %all-gather.2.cloned.1.call-done) | data formatting | bytes 4194304 | tf_op jit(solution)/shard_map/all_gather | solution.py:44
  71.3 4.4 %fusion.26 = f32[128,16,128]{2,1,0:T(8,128)S(1)} fusion(bf16[128,16,64]{2,1,0:T(8,128)(2,1)S(1)} %copy.23, bf16[128,128,64]{2,1,0:T(8,128)(2,1)} %copy.24), kind=kOutput, calls=%fused_computation.43 | convolution fusion | flops 33554432 | bytes 3407872 | tf_op jit(solution)/shard_map/cik,cjk->cij/dot_general | solution.py:41
  75.7 1.6 %copy.25 = f32[128,16,128]{0,1,2:T(8,128)} copy(f32[128,16,128]{2,1,0:T(8,128)S(1)} %fusion.26) | data formatting | bytes 2097152 | tf_op jit(solution)/shard_map/cik,cjk->cij/dot_general | solution.py:41
  77.3 0.0 reduce-scatter.2.cloned.1.call-update
  77.4 0.0 copy-done.3
  77.4 0.3 fusion.2
  77.7 8.3 %reduce-scatter.2.cloned.1.call-done = f32[128,16,64]{0,1,2:T(8,128)} async-done(((f32[128,16,128]{0,1,2:T(8,128)}), f32[128,16,64]{0,1,2:T(8,128)}) %reduce-scatter.2.cloned.1.call-update) | async-done | bytes 524304 | tf_op jit(solution)/shard_map/reduce_scatter | solution.py:47
  86.0 1.2 %reduce_sum.38 = f32[16,64]{0,1:T(8,128)S(1)} reduce(f32[128,16,64]{0,1,2:T(8,128)} %reduce-scatter.2.cloned.1.call-done, f32[]{:T(128)} %constant.11.clone.1), dimensions={0}, to_apply=%region_3.0 | reduce | flops 130048 | bytes 528388 | tf_op jit(solution)/shard_map/reduce_sum | solution.py:8
  87.2 0.1 copy.26
  87.3 0.1 copy.27
  87.4 1.4 %multiply_reduce_fusion = f32[16,64]{0,1:T(8,128)S(1)} fusion(f32[128,16,64]{0,1,2:T(8,128)} %reduce-scatter.2.cloned.1.call-done, f32[16,64]{0,1:T(8,128)S(1)} %copy.27), kind=kLoop, calls=%fused_computation.28 | loop fusion | flops 392192 | bytes 532480 | tf_op jit(solution)/shard_map/reduce_sum | solution.py:10
  88.8 0.1 copy.28
  88.9 0.1 copy.29
  89.0 0.0 copy-done.2
  89.0 1.4 %fusion.19 = bf16[16,64,128]{2,0,1:T(8,128)(2,1)S(1)} fusion(f32[128,16,64]{0,1,2:T(8,128)} %reduce-scatter.2.cloned.1.call-done, f32[128]{0:T(128)S(1)} %copy-done.2, f32[16,64]{0,1:T(8,128)S(1)} %copy.29, f32[16,64]{0,1:T(8,128)S(1)} %copy.27), kind=kLoop, calls=%fused_computation.29 | loop fusion | flops 524288 | bytes 795136 | tf_op jit(solution)/shard_map/transpose | solution.py:49
  90.4 0.0 copy-done.1
  90.4 0.9 fusion.3
  (7 shorter events, 0.0 us)
Async XLA Ops:
  6.5 5.4 %copy-start = (bf16[128,512]{1,0:T(8,128)(2,1)S(1)}, bf16[128,512]{1,0:T(8,128)(2,1)}, u32[]{:S(2)}) copy-start(bf16[128,512]{1,0:T(8,128)(2,1)} %param.9) | copy-start | bytes 393220
  6.5 57.3 %all-gather.2.cloned.1.call-start = ((), (), s32[]{:S(2)}) async-start(), calls=%async_computation.1 | async-start | bytes 2359296 | tf_op jit(solution)/shard_map/all_gather | solution.py:44
  13.4 72.6 %reduce-scatter.2.cloned.1.call-start = ((), (), s32[]{:S(2)}) async-start(), calls=%async_computation.2 | async-start | bytes 1572864 | tf_op jit(solution)/shard_map/reduce_scatter | solution.py:47
  71.3 6.1 %copy-start.3 = (bf16[128,128]{1,0:T(8,128)(2,1)S(1)}, bf16[128,128]{1,0:T(8,128)(2,1)}, u32[]{:S(2)}) copy-start(bf16[128,128]{1,0:T(8,128)(2,1)} %param.10) | copy-start | bytes 98308
  75.7 13.3 %copy-start.2 = (f32[128]{0:T(128)S(1)}, f32[128]{0:T(128)}, u32[]{:S(2)}) copy-start(f32[128]{0:T(128)} %param.13) | copy-start | bytes 1540
  75.7 14.7 %copy-start.1 = (bf16[128,128]{1,0:T(8,128)(2,1)S(1)}, bf16[128,128]{1,0:T(8,128)(2,1)}, u32[]{:S(2)}) copy-start(bf16[128,128]{1,0:T(8,128)(2,1)} %param.11) | copy-start | bytes 98308
Sparse Core Ops, SparseCore 0:
  13.5 50.2 all-gather.1
  77.5 8.4 reduce-scatter.1
where the time goes:
time: 98.9 us; the launch traced here: 98.1 us
  waiting for transfers between devices  58.3 us (59%)
  between operations  13.5 us (14%)
  other arithmetic  10.4 us (11%)
  local copies, waits for them, and re-layouts  9.81 us (10%)
  matrix products  6.05 us (6%)
    all_gather x1, waiting for transfers between devices, body(): lax.all_gather(right_major, 'row', axis=1, tiled=True)  49.9 us
    reduce_scatter x1, waiting for transfers between devices, body(): lax.psum_scatter(partial_sum, 'col', scatter_dimension=2, tiled=True)  8.33 us
    all_gather x1, local copies, waits for them, and re-layouts, body(): lax.all_gather(right_major, 'row', axis=1, tiled=True)  7.44 us
    dot_general x1, matrix products, body(): jnp.einsum('cik,cjk->cij', left_major, lax.all_gather(right_major, 'row',...  4.44 us
    reduce_sum x2, other arithmetic, layer_norm(): spread = jnp.mean(shifted * shifted, axis=along, keepdims=True)  2.75 us
    reduce_sum x2, other arithmetic, layer_norm(): centre = jnp.mean(inputs, axis=along, keepdims=True)  2.41 us
  transfers between devices with their start and end apart: 2, of which 2 were waited for; matrix products, arithmetic and copies ran while one was open for 1% of the time, Pallas kernels for 0%

commit v1 on v0

--- a/solution.py
+++ b/solution.py
@@ -1,7 +1,16 @@
 import jax
 import jax.numpy as jnp
 from jax import lax
+from jax.experimental import pallas as pl
+from jax.experimental.pallas import tpu as pltpu
 from jax.sharding import PartitionSpec as P
+
+MESH = pl.DeviceIdType.MESH
+F32 = jnp.float32
+BF16 = jnp.bfloat16
+NY = 2
+PIECES = 2
+HALF = 8
 
 
 def layer_norm(inputs, scales, along):
@@ -53,8 +62,281 @@
     return (out_gate * projected_out).astype(jnp.bfloat16)
 
 
+def kernel(x_ref, mask_ref, wp_ref, wg_ref, wo_ref, gin_ref, gout_ref, out_ref,
+           normed, cells, mcol, rbuf, lbuf, lf32, acc, gate, nsend, nout,
+           r_up, r_down, r_sib, r_recv, l_send, l_recv, n_send, n_recv):
+    rows, keys, chan = x_ref.shape
+    row = lax.axis_index("row")
+    q = lax.axis_index("col")
+    nz = lax.axis_size("row") // NY
+    z, y = row // NY, row % NY
+    sib = 1 - q
+    ynb = z * NY + (1 - y)
+    per_core = nz // 2
+    home = z // per_core
+    slot_own = jnp.where(q == home, z - per_core * q, per_core)
+    piece = keys // PIECES
+
+    barrier = pltpu.get_barrier_semaphore()
+
+    def greet(r, c):
+        pl.semaphore_signal(barrier, inc=1, device_id={"row": r, "col": c}, device_id_type=MESH)
+
+    greet(row, sib)
+    greet(ynb, q)
+
+    @pl.when(z > 0)
+    def _():
+        greet(row - NY, q)
+
+    @pl.when(z < nz - 1)
+    def _():
+        greet(row + NY, q)
+
+    def r_copy(slot, half, p, to_row, to_col, sem, from_slot=None):
+        where = pl.ds(pl.multiple_of(p * piece, piece), piece)
+        src = slot if from_slot is None else from_slot
+        return pltpu.make_async_remote_copy(
+            src_ref=rbuf.at[src, half, where], dst_ref=rbuf.at[slot, half, where],
+            send_sem=sem, recv_sem=r_recv.at[slot, half, p],
+            device_id={"row": to_row, "col": to_col}, device_id_type=MESH)
+
+    def up(slot, half, p):
+        return r_copy(slot, half, p, row + NY, q, r_up.at[slot, half, p])
+
+    def down(slot, half, p):
+        return r_copy(slot, half, p, row - NY, q, r_down.at[slot, half, p])
+
+    def to_sib(p):
+        return r_copy(z - per_core * home, q, p, row, sib, r_sib.at[p], from_slot=per_core)
+
+    def forward(slot, half, p, source, act):
+        @pl.when((z >= source) & (z < nz - 1))
+        def _():
+            act(up(slot, half, p))
+
+        @pl.when((z <= source) & (z > 0))
+        def _():
+            act(down(slot, half, p))
+
+    def l_copy(i):
+        src = (0, q) if i < 2 else (1, q)
+        dst = (0, q) if i == 0 else (1, q)
+        dev = {"row": ynb, "col": q} if i == 1 else {"row": row, "col": sib}
+        return pltpu.make_async_remote_copy(
+            src_ref=lbuf.at[src[0], src[1]], dst_ref=lbuf.at[dst[0], dst[1]],
+            send_sem=l_send.at[i], recv_sem=l_recv.at[i], device_id=dev, device_id_type=MESH)
+
+    def n_copy(rel):
+        return pltpu.make_async_remote_copy(
+            src_ref=nsend.at[rel], dst_ref=nout.at[rel * NY + y],
+            send_sem=n_send.at[rel], recv_sem=n_recv.at[rel],
+            device_id={"row": ynb, "col": q}, device_id_type=MESH)
+
+    tokens = mask_ref.shape[1]
+    mcol[...] = jnp.broadcast_to(mask_ref[...].astype(F32), (chan, tokens)).T
+    mrow = mcol[pl.ds(pl.multiple_of(row * rows, rows), rows), :]
+
+    def project(p, column):
+        n = normed[:, p * piece:(p + 1) * piece, :].reshape(rows * piece, chan)
+        both = jnp.dot(n, wp_ref[:, column:column + 2 * chan], preferred_element_type=F32)
+        cells[...] = jax.nn.sigmoid(both[:, :chan]) * both[:, chan:]
+
+    def masked(p, k):
+        key = mcol[pl.ds(q * keys + p * piece + k, 1), :]
+        return (cells[pl.ds(k, rows, stride=piece), :] * (mrow * key)).astype(BF16)
+
+    def norm_rows(v, g):
+        centre = jnp.mean(v, axis=-1, keepdims=True)
+        shifted = v - centre
+        spread = jnp.mean(shifted * shifted, axis=-1, keepdims=True)
+        return (shifted * lax.rsqrt(spread + 1e-05) * g).astype(BF16)
+
+    for p in range(PIECES):
+        v = x_ref[:, p * piece:(p + 1) * piece, :].astype(F32).reshape(rows * piece, chan)
+        normed[:, p * piece:(p + 1) * piece, :] = norm_rows(v, gin_ref[...]).reshape(rows, piece, chan)
+        project(p, 2 * chan)
+
+        def store_r(k, _):
+            rbuf[slot_own, q, p * piece + k] = masked(p, k)
+            return 0
+
+        lax.fori_loop(0, piece, store_r, 0, unroll=8)
+        if p == 0:
+            pl.semaphore_wait(barrier, 2 + (z > 0).astype(jnp.int32) + (z < nz - 1).astype(jnp.int32))
+
+        @pl.when(q == home)
+        def _():
+            forward(slot_own, q, p, z, lambda c: c.start())
+
+        @pl.when(q != home)
+        def _():
+            to_sib(p).start()
+
+    for p in range(PIECES):
+        project(p, 0)
+
+        def store_l(k, _):
+            v = masked(p, k)
+            lbuf[0, q, p * piece + k] = v
+            lf32[0, q, p * piece + k] = v.astype(F32)
+            return 0
+
+        lax.fori_loop(0, piece, store_l, 0, unroll=8)
+    l_copy(1).start()
+    l_copy(0).start()
+
+    for p in range(PIECES):
+        n = normed[:, p * piece:(p + 1) * piece, :].reshape(rows * piece, chan)
+        g = jax.nn.sigmoid(jnp.dot(n, wg_ref[...], preferred_element_type=F32))
+        gate[:, p * piece:(p + 1) * piece, :] = g.reshape(rows, piece, chan)
+
+    def widen(side, half):
+        def step(k, _):
+            lf32[side, half, k] = lbuf[side, half, k].astype(F32)
+            return 0
+
+        lax.fori_loop(0, keys, step, 0, unroll=8)
+
+    l_copy(0).wait_recv()
+    widen(0, sib)
+
+    def combine(side, slot, half, start, count, first):
+        def init(a):
+            return jnp.where(first, 0.0, a)
+
+        def step(k, sums):
+            right = rbuf[slot, half, start + k].astype(F32)
+            return tuple(
+                sums[i] + lf32[side, half, start + k, pl.ds(i, HALF, stride=0), :][None] * right.reshape(2, 8, chan)
+                for i in range(rows))
+
+        sums = tuple(init(acc[side, i].reshape(2, 8, chan)) for i in range(rows))
+        sums = lax.fori_loop(0, count, step, sums, unroll=4)
+        for i in range(rows):
+            acc[side, i] = sums[i].reshape(rows, chan)
+
+    def finish(side, put):
+        for b in range(0, rows, 8):
+            v = acc[side, b:b + 8].reshape(8 * rows, chan)
+            put(b, norm_rows(v, gout_ref[...]).reshape(8, rows, chan))
+
+    near = jnp.clip(z - per_core * q, 0, per_core - 1)
+    for t in range(2):
+        slot = near if t == 0 else 1 - near
+        source = per_core * q + slot
+
+        def arrive(n, _):
+            h, p = n // PIECES, n % PIECES
+            half = jnp.where(h == 0, q, sib)
+
+            @pl.when(jnp.logical_not((source == z) & (h == 0)))
+            def _():
+                up(slot, half, p).wait_recv()
+                forward(slot, half, p, source, lambda c: c.start())
+
+            combine(0, slot, half, p * piece, piece, n == 0)
+            if t == 1:
+                combine(1, slot, half, p * piece, piece, n == 0)
+            return 0
+
+        lax.fori_loop(0, 2 * PIECES, arrive, 0)
+        if t == 0:
+            l_copy(1).wait_recv()
+            l_copy(2).start()
+            widen(1, q)
+            l_copy(2).wait_recv()
+            widen(1, sib)
+            combine(1, slot, q, 0, keys, True)
+            combine(1, slot, sib, 0, keys, False)
+
+        def put_send(b, v):
+            nsend[slot, b:b + 8] = v
+
+        def put_own(b, v):
+            nout[slot * NY + y, b:b + 8] = v
+
+        finish(1, put_send)
+        n_copy(slot).start()
+        finish(0, put_own)
+
+    def emit(block, at):
+        n = nout[block].reshape(rows * rows, chan)
+        o = jnp.dot(n, wo_ref[...], preferred_element_type=F32).reshape(rows, rows, chan)
+        where = pl.ds(pl.multiple_of(at * rows, rows), rows)
+        out_ref[:, where, :] = (gate[:, where, :] * o).astype(BF16)
+
+    for t in range(2):
+        emit(t * NY + y, t * NY + y)
+    for t in range(2):
+        slot = near if t == 0 else 1 - near
+        n_copy(slot).wait_recv()
+        emit(slot * NY + 1 - y, slot * NY + 1 - y)
+
+    for i in range(3):
+        l_copy(i).wait_send()
+    for t in range(2):
+        n_copy(t).wait_send()
+
+    def drain(n, _):
+        slot, h, p = n // (2 * PIECES), (n // PIECES) % 2, n % PIECES
+        forward(slot, h, p, per_core * q + slot, lambda c: c.wait_send())
+        return 0
+
+    lax.fori_loop(0, 4 * PIECES, drain, 0)
+
+    @pl.when(q != home)
+    def _():
+        for p in range(PIECES):
+            to_sib(p).wait_send()
+
+
+def fused(pair_grid, token_mask, proj_weight, gate_weight, out_weight, in_gain, out_gain):
+    rows, keys, chan = pair_grid.shape
+    tokens = token_mask.shape[0]
+    vmem = pl.BlockSpec(memory_space=pltpu.VMEM)
+    dma = pltpu.SemaphoreType.DMA
+    return pl.pallas_call(
+        kernel,
+        out_shape=jax.ShapeDtypeStruct(pair_grid.shape, BF16),
+        in_specs=[vmem] * 7,
+        out_specs=vmem,
+        scratch_shapes=[
+            pltpu.VMEM((rows, keys, chan), BF16),
+            pltpu.VMEM((rows * keys // PIECES, chan), F32),
+            pltpu.VMEM((tokens, chan), F32),
+            pltpu.VMEM((3, 2, keys, rows, chan), BF16),
+            pltpu.VMEM((2, 2, keys, rows, chan), BF16),
+            pltpu.VMEM((2, 2, keys, rows, chan), F32),
+            pltpu.VMEM((2, rows, rows, chan), F32),
+            pltpu.VMEM((rows, keys, chan), F32),
+            pltpu.VMEM((2, rows, rows, chan), BF16),
+            pltpu.VMEM((4, rows, rows, chan), BF16),
+            dma((2, 2, PIECES)),
+            dma((2, 2, PIECES)),
+            dma((PIECES,)),
+            dma((2, 2, PIECES)),
+            dma((3,)),
+            dma((3,)),
+            dma((2,)),
+            dma((2,)),
+        ],
+        compiler_params=pltpu.CompilerParams(
+            collective_id=0, has_side_effects=True, vmem_limit_bytes=40 * 1024 * 1024),
+        cost_estimate=pl.CostEstimate(
+            flops=4 * rows * keys * 2 * keys * chan, bytes_accessed=4 * rows * keys * chan, transcendentals=0),
+    )(pair_grid, token_mask.reshape(1, tokens), proj_weight, gate_weight, out_weight,
+      in_gain.reshape(1, chan), out_gain.reshape(1, chan))
+
+
 def solution(mesh):
     placed = (P(("grp", "row"), "col", None), P("grp"), P(), P(), P(), P(), P())
+
+    def run(pair_grid, *rest):
+        rows, keys, chan = pair_grid.shape
+        small = mesh.shape["row"] == 4 * NY and rows % 16 == 0 and keys == 4 * rows
+        return (fused if small else body)(pair_grid, *rest)
+
     return jax.shard_map(
-        body, mesh=mesh, in_specs=placed, out_specs=P(("grp", "row"), "col", None), check_vma=False
+        run, mesh=mesh, in_specs=placed, out_specs=P(("grp", "row"), "col", None), check_vma=False
     )

time: 98.9 us -> 35.9 us (0.36)
  waiting for transfers between devices: 58.3 us -> 0 us
  Pallas kernels: 0 us -> 30.8 us
  between operations: 13.5 us -> 0.02 us
  other arithmetic: 10.4 us -> 0 us
  matrix products: 6.05 us -> 0 us
  local copies, waits for them, and re-layouts: 9.81 us -> 4.75 us
    all_gather x1 -> x0, waiting for transfers between devices: 49.9 us -> none  [body(): lax.all_gather(right_major, 'row', axis=1, tiled=True)]
    pallas_call x0 -> x1, Pallas kernels: none -> 30.8 us  [fused(): pl.pallas_call(kernel, out_shape=jax.ShapeDtypeStruct(pair_grid.shape, BF...]
    reduce_scatter x1 -> x0, waiting for transfers between devices: 8.33 us -> none  [body(): lax.psum_scatter(partial_sum, 'col', scatter_dimension=2, tiled=True)]
    all_gather x1 -> x0, local copies, waits for them, and re-layouts: 7.44 us -> none  [body(): lax.all_gather(right_major, 'row', axis=1, tiled=True)]
    dot_general x4 -> x0, matrix products: 6.05 us -> none  [the longest x1 4.44 us: body(): jnp.einsum('cik,cjk->cij', left_major, lax.all_gather(right_major, 'row',...]
    reduce_sum x4 -> x0, other arithmetic: 5.16 us -> none  [the longest x2 2.75 us: layer_norm(): spread = jnp.mean(shifted * shifted, axis=along, keepdims=True)]
    unnamed x8 -> x15, local copies, waits for them, and re-layouts: 0.02 us -> 4.75 us
    convert_element_type x3 -> x0, other arithmetic: 2.78 us -> none  [the longest x1 1.29 us: body(): layer_norm(pair_grid.astype(jnp.float32), in_gain, -1).astype(jnp.bfloat16)]
  transfers between devices with their start and end apart: 2 -> 0, of which waited for: 2 -> 0; matrix products, arithmetic and copies ran while one was open for 1% -> 0% of each run, Pallas kernels for 0% -> 0%
where the time goes in v1:
time: 35.9 us; the launch traced here: 35.6 us
  Pallas kernels  30.8 us (86%)
  local copies, waits for them, and re-layouts  4.75 us (13%)
    pallas_call x1, Pallas kernels, fused(): pl.pallas_call(kernel, out_shape=jax.ShapeDtypeStruct(pair_grid.shape, BF...  30.8 us
    unnamed x15, local copies, waits for them, and re-layouts  4.75 us

profile of v1, /device:TPU:1, one launch (start us, length us, event | category | flops | bytes accessed | tf_op | source)
XLA Modules:
  0.0 35.6 jit_solution(15429256595754991824)
XLA Ops:
  0.0 0.0 copy-start.4
  0.0 0.0 copy-start.5
  0.0 0.0 copy-start.6
  0.0 0.6 %copy-done.4 = s32[128]{0:T(128)S(1)} copy-done((s32[128]{0:T(128)S(1)}, s32[128]{0:T(128)}, u32[]{:S(2)}) %copy-start.4) | copy-done | bytes 536
  0.7 0.0 copy-done.5
  0.7 0.0 copy-done.6
  0.7 0.0 copy-start
  0.7 0.9 %copy-done = bf16[16,64,128]{2,1,0:T(8,128)(2,1)S(1)} copy-done((bf16[16,64,128]{2,1,0:T(8,128)(2,1)S(1)}, bf16[16,64,128]{2,1,0:T(8,128)(2,1)}, u32[]{:S(2)}) %copy-start) | copy-done | bytes 262168
  1.6 0.0 copy-start.1
  1.6 0.9 %copy-done.1 = bf16[128,512]{1,0:T(8,128)(2,1)S(1)} copy-done((bf16[128,512]{1,0:T(8,128)(2,1)S(1)}, bf16[128,512]{1,0:T(8,128)(2,1)}, u32[]{:S(2)}) %copy-start.1) | copy-done | bytes 131096
  2.5 0.0 copy-start.2
  2.5 0.8 %copy-done.2 = bf16[128,128]{1,0:T(8,128)(2,1)S(1)} copy-done((bf16[128,128]{1,0:T(8,128)(2,1)S(1)}, bf16[128,128]{1,0:T(8,128)(2,1)}, u32[]{:S(2)}) %copy-start.2) | copy-done | bytes 32792
  3.3 0.0 copy-start.3
  3.3 0.8 %copy-done.3 = bf16[128,128]{1,0:T(8,128)(2,1)S(1)} copy-done((bf16[128,128]{1,0:T(8,128)(2,1)S(1)}, bf16[128,128]{1,0:T(8,128)(2,1)}, u32[]{:S(2)}) %copy-start.3) | copy-done | bytes 32792
  4.1 30.8 %shard_map.73 = bf16[16,64,128]{2,1,0:T(8,128)(2,1)S(1)} custom-call(bf16[16,64,128]{2,1,0:T(8,128)(2,1)S(1)} %copy-done, s32[1,128]{1,0:T(1,128)S(1)} %bitcast.3, bf16[128,512]{1,0:T(8,128)(2,1)S(1)} %copy-done.1, bf16[128,128]{1,0:T(8,128)(2,1)S(1)} %copy-done.2, bf16[128,128]{1,0:T(8,128)(2,1)S(1)} %copy-done.3, f32[1,128]{1,0:T(1,128)S(1)} %bitcast.4, ...), custom_call_target="tpu_custom_call" | custom-call | flops 67108864 | bytes 524288 | tf_op jit(solution)/shard_map/pallas_call | solution.py:299
  34.9 0.7 %copy.9 = bf16[16,64,128]{2,1,0:T(8,128)(2,1)} copy(bf16[16,64,128]{2,1,0:T(8,128)(2,1)S(1)} %shard_map.73) | data formatting | bytes 524288
Async XLA Ops:
  0.0 0.7 %copy-start.4 = (s32[128]{0:T(128)S(1)}, s32[128]{0:T(128)}, u32[]{:S(2)}) copy-start(s32[128]{0:T(128)} %param.8) | copy-start | bytes 1540
  0.0 0.7 %copy-start.5 = (f32[128]{0:T(128)S(1)}, f32[128]{0:T(128)}, u32[]{:S(2)}) copy-start(f32[128]{0:T(128)} %param.12) | copy-start | bytes 1540
  0.0 0.7 %copy-start.6 = (f32[128]{0:T(128)S(1)}, f32[128]{0:T(128)}, u32[]{:S(2)}) copy-start(f32[128]{0:T(128)} %param.13) | copy-start | bytes 1540
  0.7 0.9 %copy-start = (bf16[16,64,128]{2,1,0:T(8,128)(2,1)S(1)}, bf16[16,64,128]{2,1,0:T(8,128)(2,1)}, u32[]{:S(2)}) copy-start(bf16[16,64,128]{2,1,0:T(8,128)(2,1)} %x_ref.1) | copy-start | bytes 786436
  1.6 0.9 %copy-start.1 = (bf16[128,512]{1,0:T(8,128)(2,1)S(1)}, bf16[128,512]{1,0:T(8,128)(2,1)}, u32[]{:S(2)}) copy-start(bf16[128,512]{1,0:T(8,128)(2,1)} %wp_ref.1) | copy-start | bytes 393220
  2.5 0.8 %copy-start.2 = (bf16[128,128]{1,0:T(8,128)(2,1)S(1)}, bf16[128,128]{1,0:T(8,128)(2,1)}, u32[]{:S(2)}) copy-start(bf16[128,128]{1,0:T(8,128)(2,1)} %wg_ref.1) | copy-start | bytes 98308
  3.3 0.8 %copy-start.3 = (bf16[128,128]{1,0:T(8,128)(2,1)S(1)}, bf16[128,128]{1,0:T(8,128)(2,1)}, u32[]{:S(2)}) copy-start(bf16[128,128]{1,0:T(8,128)(2,1)} %wo_ref.1) | copy-start | bytes 98308

commit v2 on v1

--- a/solution.py
+++ b/solution.py
@@ -9,8 +9,8 @@
 F32 = jnp.float32
 BF16 = jnp.bfloat16
 NY = 2
-PIECES = 2
-HALF = 8
+PIECES = 4
+VMEM_BYTES = 63 * 1024 * 1024
 
 
 def layer_norm(inputs, scales, along):
@@ -62,7 +62,8 @@
     return (out_gate * projected_out).astype(jnp.bfloat16)
 
 
-def kernel(x_ref, mask_ref, wp_ref, wg_ref, wo_ref, gin_ref, gout_ref, out_ref,
+def kernel(x_hbm, mask_hbm, wp_hbm, wg_hbm, wo_hbm, gin_hbm, gout_hbm, out_ref,
+           x_ref, mask_ref, wp_ref, wg_ref, wo_ref, gin_ref, gout_ref, load_sem,
            normed, cells, mcol, rbuf, lbuf, lf32, acc, gate, nsend, nout,
            r_up, r_down, r_sib, r_recv, l_send, l_recv, n_send, n_recv):
     rows, keys, chan = x_ref.shape
@@ -77,6 +78,12 @@
     slot_own = jnp.where(q == home, z - per_core * q, per_core)
     piece = keys // PIECES
 
+    hbm = (mask_hbm, gin_hbm, x_hbm, wp_hbm, wg_hbm, wo_hbm, gout_hbm)
+    local = (mask_ref, gin_ref, x_ref, wp_ref, wg_ref, wo_ref, gout_ref)
+    loads = [pltpu.make_async_copy(a, b, load_sem.at[i]) for i, (a, b) in enumerate(zip(hbm, local))]
+    for load in loads:
+        load.start()
+
     barrier = pltpu.get_barrier_semaphore()
 
     def greet(r, c):
@@ -133,6 +140,7 @@
             send_sem=n_send.at[rel], recv_sem=n_recv.at[rel],
             device_id={"row": ynb, "col": q}, device_id_type=MESH)
 
+    loads[0].wait()
     tokens = mask_ref.shape[1]
     mcol[...] = jnp.broadcast_to(mask_ref[...].astype(F32), (chan, tokens)).T
     mrow = mcol[pl.ds(pl.multiple_of(row * rows, rows), rows), :]
@@ -152,6 +160,8 @@
         spread = jnp.mean(shifted * shifted, axis=-1, keepdims=True)
         return (shifted * lax.rsqrt(spread + 1e-05) * g).astype(BF16)
 
+    for load in loads[1:4]:
+        load.wait()
     for p in range(PIECES):
         v = x_ref[:, p * piece:(p + 1) * piece, :].astype(F32).reshape(rows * piece, chan)
         normed[:, p * piece:(p + 1) * piece, :] = norm_rows(v, gin_ref[...]).reshape(rows, piece, chan)
@@ -183,95 +193,139 @@
             return 0
 
         lax.fori_loop(0, piece, store_l, 0, unroll=8)
+    l_copy(0).start()
     l_copy(1).start()
-    l_copy(0).start()
-
+
+    def widen(side, half):
+        def step(k, _):
+            lf32[side, half, k] = lbuf[side, half, k].astype(F32)
+            return 0
+
+        lax.fori_loop(0, keys, step, 0, unroll=8)
+
+    l_copy(0).wait_recv()
+    widen(0, sib)
+
+    def combine(side, slot, half, start, count, first):
+        def init(a):
+            return jnp.where(first, 0.0, a)
+
+        def step(k, sums):
+            right = rbuf[slot, half, start + k].astype(F32).reshape(2, 8, chan)
+            return tuple(
+                sums[i] + lf32[side, half, start + k, pl.ds(i, 8, stride=0), :][None] * right
+                for i in range(rows))
+
+        sums = tuple(init(acc[side, slot, i].reshape(2, 8, chan)) for i in range(rows))
+        sums = lax.fori_loop(0, count, step, sums, unroll=4)
+        for i in range(rows):
+            acc[side, slot, i] = sums[i].reshape(rows, chan)
+
+    def finish(side, slot, put):
+        for b in range(0, rows, 8):
+            v = acc[side, slot, b:b + 8].reshape(8 * rows, chan)
+            put(b, norm_rows(v, gout_ref[...]).reshape(8, rows, chan))
+
+    near = jnp.clip(z - per_core * q, 0, per_core - 1)
+    far = 1 - near
+    at_end = (z == 0) | (z == nz - 1)
+
+    def arrive(slot, n, then):
+        source = per_core * q + slot
+        h, p = n // PIECES, n % PIECES
+        half = jnp.where(h == 0, q, sib)
+
+        @pl.when(jnp.logical_not((source == z) & (h == 0)))
+        def _():
+            up(slot, half, p).wait_recv()
+            forward(slot, half, p, source, lambda c: c.start())
+
+        combine(0, slot, half, p * piece, piece, n == 0)
+        then(half, p)
+        return 0
+
+    def neighbour_left():
+        l_copy(1).wait_recv()
+        l_copy(2).start()
+        widen(1, q)
+        l_copy(2).wait_recv()
+        widen(1, sib)
+
+    def put_send(slot):
+        def put(b, v):
+            nsend[slot, b:b + 8] = v
+
+        return put
+
+    def put_own(slot):
+        def put(b, v):
+            nout[slot * NY + y, b:b + 8] = v
+
+        return put
+
+    def emit(block):
+        n = nout[block].reshape(rows * rows, chan)
+        o = jnp.dot(n, wo_ref[...], preferred_element_type=F32).reshape(rows, rows, chan)
+        where = pl.ds(pl.multiple_of(block * rows, rows), rows)
+        out_ref[:, where, :] = (gate[:, where, :] * o).astype(BF16)
+
+    def close_neighbour(slot):
+        finish(1, slot, put_send(slot))
+        n_copy(slot).start()
+
+    def close_own(slot):
+        finish(0, slot, put_own(slot))
+        emit(slot * NY + y)
+
+    def close_other(slot):
+        n_copy(slot).wait_recv()
+        emit(slot * NY + 1 - y)
+
+    lax.fori_loop(0, 2 * PIECES, lambda n, _: arrive(near, n, lambda half, p: None), 0)
+
+    for load in loads[4:]:
+        load.wait()
     for p in range(PIECES):
         n = normed[:, p * piece:(p + 1) * piece, :].reshape(rows * piece, chan)
         g = jax.nn.sigmoid(jnp.dot(n, wg_ref[...], preferred_element_type=F32))
         gate[:, p * piece:(p + 1) * piece, :] = g.reshape(rows, piece, chan)
 
-    def widen(side, half):
-        def step(k, _):
-            lf32[side, half, k] = lbuf[side, half, k].astype(F32)
-            return 0
-
-        lax.fori_loop(0, keys, step, 0, unroll=8)
-
-    l_copy(0).wait_recv()
-    widen(0, sib)
-
-    def combine(side, slot, half, start, count, first):
-        def init(a):
-            return jnp.where(first, 0.0, a)
-
-        def step(k, sums):
-            right = rbuf[slot, half, start + k].astype(F32)
-            return tuple(
-                sums[i] + lf32[side, half, start + k, pl.ds(i, HALF, stride=0), :][None] * right.reshape(2, 8, chan)
-                for i in range(rows))
-
-        sums = tuple(init(acc[side, i].reshape(2, 8, chan)) for i in range(rows))
-        sums = lax.fori_loop(0, count, step, sums, unroll=4)
-        for i in range(rows):
-            acc[side, i] = sums[i].reshape(rows, chan)
-
-    def finish(side, put):
-        for b in range(0, rows, 8):
-            v = acc[side, b:b + 8].reshape(8 * rows, chan)
-            put(b, norm_rows(v, gout_ref[...]).reshape(8, rows, chan))
-
-    near = jnp.clip(z - per_core * q, 0, per_core - 1)
-    for t in range(2):
-        slot = near if t == 0 else 1 - near
-        source = per_core * q + slot
-
-        def arrive(n, _):
-            h, p = n // PIECES, n % PIECES
-            half = jnp.where(h == 0, q, sib)
-
-            @pl.when(jnp.logical_not((source == z) & (h == 0)))
+    close_own(near)
+
+    @pl.when(at_end)
+    def _():
+        neighbour_left()
+        combine(1, near, q, 0, keys, True)
+        combine(1, near, sib, 0, keys, False)
+        close_neighbour(near)
+
+    def second(n, _):
+        def then(half, p):
+            @pl.when(at_end)
             def _():
-                up(slot, half, p).wait_recv()
-                forward(slot, half, p, source, lambda c: c.start())
-
-            combine(0, slot, half, p * piece, piece, n == 0)
-            if t == 1:
-                combine(1, slot, half, p * piece, piece, n == 0)
-            return 0
-
-        lax.fori_loop(0, 2 * PIECES, arrive, 0)
-        if t == 0:
-            l_copy(1).wait_recv()
-            l_copy(2).start()
-            widen(1, q)
-            l_copy(2).wait_recv()
-            widen(1, sib)
-            combine(1, slot, q, 0, keys, True)
-            combine(1, slot, sib, 0, keys, False)
-
-        def put_send(b, v):
-            nsend[slot, b:b + 8] = v
-
-        def put_own(b, v):
-            nout[slot * NY + y, b:b + 8] = v
-
-        finish(1, put_send)
-        n_copy(slot).start()
-        finish(0, put_own)
-
-    def emit(block, at):
-        n = nout[block].reshape(rows * rows, chan)
-        o = jnp.dot(n, wo_ref[...], preferred_element_type=F32).reshape(rows, rows, chan)
-        where = pl.ds(pl.multiple_of(at * rows, rows), rows)
-        out_ref[:, where, :] = (gate[:, where, :] * o).astype(BF16)
-
-    for t in range(2):
-        emit(t * NY + y, t * NY + y)
-    for t in range(2):
-        slot = near if t == 0 else 1 - near
-        n_copy(slot).wait_recv()
-        emit(slot * NY + 1 - y, slot * NY + 1 - y)
+                combine(1, far, half, p * piece, piece, n == 0)
+
+            @pl.when(jnp.logical_not(at_end) & (n >= PIECES))
+            def _():
+                combine(1, near, q, p * piece, piece, n == PIECES)
+                combine(1, near, sib, p * piece, piece, False)
+                combine(1, far, q, p * piece, piece, n == PIECES)
+                combine(1, far, sib, p * piece, piece, False)
+
+        pl.when(jnp.logical_not(at_end) & (n == PIECES))(neighbour_left)
+        return arrive(far, n, then)
+
+    lax.fori_loop(0, 2 * PIECES, second, 0)
+
+    @pl.when(jnp.logical_not(at_end))
+    def _():
+        close_neighbour(near)
+
+    close_neighbour(far)
+
+    close_own(far)
+    close_other(near)
+    close_other(far)
 
     for i in range(3):
         l_copy(i).wait_send()
@@ -296,19 +350,23 @@
     tokens = token_mask.shape[0]
     vmem = pl.BlockSpec(memory_space=pltpu.VMEM)
     dma = pltpu.SemaphoreType.DMA
+    operands = (pair_grid, token_mask.reshape(1, tokens), proj_weight, gate_weight, out_weight,
+                in_gain.reshape(1, chan), out_gain.reshape(1, chan))
     return pl.pallas_call(
         kernel,
         out_shape=jax.ShapeDtypeStruct(pair_grid.shape, BF16),
-        in_specs=[vmem] * 7,
+        in_specs=[pl.BlockSpec(memory_space=pltpu.HBM)] * 7,
         out_specs=vmem,
         scratch_shapes=[
+            *(pltpu.VMEM(a.shape, a.dtype) for a in operands),
+            dma((7,)),
             pltpu.VMEM((rows, keys, chan), BF16),
             pltpu.VMEM((rows * keys // PIECES, chan), F32),
             pltpu.VMEM((tokens, chan), F32),
             pltpu.VMEM((3, 2, keys, rows, chan), BF16),
             pltpu.VMEM((2, 2, keys, rows, chan), BF16),
             pltpu.VMEM((2, 2, keys, rows, chan), F32),
-            pltpu.VMEM((2, rows, rows, chan), F32),
+            pltpu.VMEM((2, 2, rows, rows, chan), F32),
             pltpu.VMEM((rows, keys, chan), F32),
             pltpu.VMEM((2, rows, rows, chan), BF16),
             pltpu.VMEM((4, rows, rows, chan), BF16),
@@ -322,11 +380,10 @@
             dma((2,)),
         ],
         compiler_params=pltpu.CompilerParams(
-            collective_id=0, has_side_effects=True, vmem_limit_bytes=40 * 1024 * 1024),
+            collective_id=0, has_side_effects=True, vmem_limit_bytes=VMEM_BYTES),
         cost_estimate=pl.CostEstimate(
             flops=4 * rows * keys * 2 * keys * chan, bytes_accessed=4 * rows * keys * chan, transcendentals=0),
-    )(pair_grid, token_mask.reshape(1, tokens), proj_weight, gate_weight, out_weight,
-      in_gain.reshape(1, chan), out_gain.reshape(1, chan))
+    )(*operands)
 
 
 def solution(mesh):

time: 35.9 us -> 32.3 us (0.90)
  local copies, waits for them, and re-layouts: 4.75 us -> 1.67 us
    unnamed x15 -> x1, local copies, waits for them, and re-layouts: 4.75 us -> 1.67 us
where the time goes in v2:
time: 32.3 us; the launch traced here: 32.2 us
  Pallas kernels  30.5 us (94%)
  local copies, waits for them, and re-layouts  1.67 us (5%)
    pallas_call x1, Pallas kernels, fused(): pl.pallas_call(kernel, out_shape=jax.ShapeDtypeStruct(pair_grid.shape, BF...  30.5 us
    unnamed x1, local copies, waits for them, and re-layouts  1.67 us

profile of v2, /device:TPU:1, one launch (start us, length us, event | category | flops | bytes accessed | tf_op | source)
XLA Modules:
  0.0 32.2 jit_solution(2863605641643894099)
XLA Ops:
  0.0 30.5 %shard_map.73 = bf16[16,64,128]{2,1,0:T(8,128)(2,1)} custom-call(bf16[16,64,128]{2,1,0:T(8,128)(2,1)} %x_hbm.1, s32[1,128]{1,0:T(1,128)} %bitcast.3, bf16[128,512]{1,0:T(8,128)(2,1)} %wp_hbm.1, bf16[128,128]{1,0:T(8,128)(2,1)} %wg_hbm.1, bf16[128,128]{1,0:T(8,128)(2,1)} %wo_hbm.1, f32[1,128]{1,0:T(1,128)} %bitcast.4, f32[1,128]{1,0:T(1,128)} %bitcast.5), custom_call_target="tpu_custom_call" | custom-call | flops 67108864 | bytes 524288 | tf_op jit(solution)/shard_map/pallas_call | solution.py:355
  30.5 1.7 %copy.9 = bf16[16,64,128]{2,1,0:T(8,128)(2,1)} copy(bf16[16,64,128]{2,1,0:T(8,128)(2,1)} %shard_map.73) | data formatting | bytes 524288

commit v3 on v2

--- a/solution.py
+++ b/solution.py
@@ -203,9 +203,6 @@
 
         lax.fori_loop(0, keys, step, 0, unroll=8)
 
-    l_copy(0).wait_recv()
-    widen(0, sib)
-
     def combine(side, slot, half, start, count, first):
         def init(a):
             return jnp.where(first, 0.0, a)
@@ -240,13 +237,17 @@
             up(slot, half, p).wait_recv()
             forward(slot, half, p, source, lambda c: c.start())
 
-        combine(0, slot, half, p * piece, piece, n == 0)
         then(half, p)
         return 0
 
-    def neighbour_left():
+    def pass_left():
         l_copy(1).wait_recv()
         l_copy(2).start()
+
+    early = at_end & (q != home)
+
+    def neighbour_left():
+        pl.when(jnp.logical_not(early))(pass_left)
         widen(1, q)
         l_copy(2).wait_recv()
         widen(1, sib)
@@ -281,19 +282,27 @@
         n_copy(slot).wait_recv()
         emit(slot * NY + 1 - y)
 
+    pl.when(early)(pass_left)
     lax.fori_loop(0, 2 * PIECES, lambda n, _: arrive(near, n, lambda half, p: None), 0)
 
-    for load in loads[4:]:
-        load.wait()
-    for p in range(PIECES):
-        n = normed[:, p * piece:(p + 1) * piece, :].reshape(rows * piece, chan)
-        g = jax.nn.sigmoid(jnp.dot(n, wg_ref[...], preferred_element_type=F32))
-        gate[:, p * piece:(p + 1) * piece, :] = g.reshape(rows, piece, chan)
-
-    close_own(near)
+    l_copy(0).wait_recv()
+    widen(0, sib)
+    combine(0, near, q, 0, keys, True)
+    combine(0, near, sib, 0, keys, False)
+
+    def gate_and_near():
+        for load in loads[4:]:
+            load.wait()
+        for p in range(PIECES):
+            n = normed[:, p * piece:(p + 1) * piece, :].reshape(rows * piece, chan)
+            g = jax.nn.sigmoid(jnp.dot(n, wg_ref[...], preferred_element_type=F32))
+            gate[:, p * piece:(p + 1) * piece, :] = g.reshape(rows, piece, chan)
+
+        close_own(near)
 
     @pl.when(at_end)
     def _():
+        gate_and_near()
         neighbour_left()
         combine(1, near, q, 0, keys, True)
         combine(1, near, sib, 0, keys, False)
@@ -301,6 +310,8 @@
 
     def second(n, _):
         def then(half, p):
+            combine(0, far, half, p * piece, piece, n == 0)
+
             @pl.when(at_end)
             def _():
                 combine(1, far, half, p * piece, piece, n == 0)
@@ -312,7 +323,11 @@
                 combine(1, far, q, p * piece, piece, n == PIECES)
                 combine(1, far, sib, p * piece, piece, False)
 
-        pl.when(jnp.logical_not(at_end) & (n == PIECES))(neighbour_left)
+        @pl.when(jnp.logical_not(at_end) & (n == PIECES))
+        def _():
+            gate_and_near()
+            neighbour_left()
+
         return arrive(far, n, then)
 
     lax.fori_loop(0, 2 * PIECES, second, 0)

time: 32.3 us -> 31.6 us (0.978)
  Pallas kernels: 30.5 us -> 29.7 us
    pallas_call x1, Pallas kernels: 30.5 us -> 29.7 us  [fused(): pl.pallas_call(kernel, out_shape=jax.ShapeDtypeStruct(pair_grid.shape, BF...]
where the time goes in v3:
time: 31.6 us; the launch traced here: 31.4 us
  Pallas kernels  29.7 us (94%)
  local copies, waits for them, and re-layouts  1.67 us (5%)
    pallas_call x1, Pallas kernels, fused(): pl.pallas_call(kernel, out_shape=jax.ShapeDtypeStruct(pair_grid.shape, BF...  29.7 us
    unnamed x1, local copies, waits for them, and re-layouts  1.67 us

profile of v3, /device:TPU:1, one launch (start us, length us, event | category | flops | bytes accessed | tf_op | source)
XLA Modules:
  0.0 31.4 jit_solution(17767364664986101671)
XLA Ops:
  0.0 29.7 %shard_map.73 = bf16[16,64,128]{2,1,0:T(8,128)(2,1)} custom-call(bf16[16,64,128]{2,1,0:T(8,128)(2,1)} %x_hbm.1, s32[1,128]{1,0:T(1,128)} %bitcast.3, bf16[128,512]{1,0:T(8,128)(2,1)} %wp_hbm.1, bf16[128,128]{1,0:T(8,128)(2,1)} %wg_hbm.1, bf16[128,128]{1,0:T(8,128)(2,1)} %wo_hbm.1, f32[1,128]{1,0:T(1,128)} %bitcast.4, f32[1,128]{1,0:T(1,128)} %bitcast.5), custom_call_target="tpu_custom_call" | custom-call | flops 67108864 | bytes 524288 | tf_op jit(solution)/shard_map/pallas_call | solution.py:370
  29.7 1.7 %copy.9 = bf16[16,64,128]{2,1,0:T(8,128)(2,1)} copy(bf16[16,64,128]{2,1,0:T(8,128)(2,1)} %shard_map.73) | data formatting | bytes 524288

commit v4 on v3

--- a/solution.py
+++ b/solution.py
@@ -300,7 +300,9 @@
 
         close_own(near)
 
-    @pl.when(at_end)
+    ahead = at_end | (q != home)
+
+    @pl.when(ahead)
     def _():
         gate_and_near()
         neighbour_left()
@@ -312,28 +314,21 @@
         def then(half, p):
             combine(0, far, half, p * piece, piece, n == 0)
 
-            @pl.when(at_end)
+            @pl.when(ahead)
             def _():
                 combine(1, far, half, p * piece, piece, n == 0)
 
-            @pl.when(jnp.logical_not(at_end) & (n >= PIECES))
-            def _():
-                combine(1, near, q, p * piece, piece, n == PIECES)
-                combine(1, near, sib, p * piece, piece, False)
-                combine(1, far, q, p * piece, piece, n == PIECES)
-                combine(1, far, sib, p * piece, piece, False)
-
-        @pl.when(jnp.logical_not(at_end) & (n == PIECES))
-        def _():
-            gate_and_near()
-            neighbour_left()
-
         return arrive(far, n, then)
 
     lax.fori_loop(0, 2 * PIECES, second, 0)
 
-    @pl.when(jnp.logical_not(at_end))
+    @pl.when(jnp.logical_not(ahead))
     def _():
+        gate_and_near()
+        neighbour_left()
+        for slot in (near, far):
+            combine(1, slot, q, 0, keys, True)
+            combine(1, slot, sib, 0, keys, False)
         close_neighbour(near)
 
     close_neighbour(far)

time: 31.6 us -> 30.9 us (0.978)
  Pallas kernels: 29.7 us -> 29 us
    pallas_call x1, Pallas kernels: 29.7 us -> 29 us  [fused(): pl.pallas_call(kernel, out_shape=jax.ShapeDtypeStruct(pair_grid.shape, BF...]
where the time goes in v4:
time: 30.9 us; the launch traced here: 30.7 us
  Pallas kernels  29 us (94%)
  local copies, waits for them, and re-layouts  1.67 us (5%)
    pallas_call x1, Pallas kernels, fused(): pl.pallas_call(kernel, out_shape=jax.ShapeDtypeStruct(pair_grid.shape, BF...  29 us
    unnamed x1, local copies, waits for them, and re-layouts  1.67 us

profile of v4, /device:TPU:1, one launch (start us, length us, event | category | flops | bytes accessed | tf_op | source)
XLA Modules:
  0.0 30.7 jit_solution(5407242027394276410)
XLA Ops:
  0.0 29.0 %shard_map.73 = bf16[16,64,128]{2,1,0:T(8,128)(2,1)} custom-call(bf16[16,64,128]{2,1,0:T(8,128)(2,1)} %x_hbm.1, s32[1,128]{1,0:T(1,128)} %bitcast.3, bf16[128,512]{1,0:T(8,128)(2,1)} %wp_hbm.1, bf16[128,128]{1,0:T(8,128)(2,1)} %wg_hbm.1, bf16[128,128]{1,0:T(8,128)(2,1)} %wo_hbm.1, f32[1,128]{1,0:T(1,128)} %bitcast.4, f32[1,128]{1,0:T(1,128)} %bitcast.5), custom_call_target="tpu_custom_call" | custom-call | flops 67108864 | bytes 524288 | tf_op jit(solution)/shard_map/pallas_call | solution.py:365
  29.1 1.7 %copy.9 = bf16[16,64,128]{2,1,0:T(8,128)(2,1)} copy(bf16[16,64,128]{2,1,0:T(8,128)(2,1)} %shard_map.73) | data formatting | bytes 524288
